TPU v7x, 32 devices: a whole 2x2x4 slice. The times are simulated.
32 devices in a mesh: grp: 2 (over y), blk: 8 (over z, core), red: 2 (over x), sub: 1.
Axes of the slice: x: 2, y: 2, z: 4, core: 2. Of those that a mesh axis runs over, the one named last changes fastest.
Arguments:
- tokens: bfloat16 [256, 8192], P(('grp', 'blk'), ('red', 'sub')), parts along dimension 0, may hold values from -12 to 12
- input_gain: bfloat16 [8192], replicated, may hold values from 0.5 to 1.5
- in_weight: bfloat16 [2, 8192, 16384], P(None, None, ('blk', 'red', 'sub')), may hold values from -0.0625 to 0.0625
- conv_weight: bfloat16 [4, 16384], P(None, ('blk', 'red', 'sub')), may hold values from -2.5 to 2.5
- conv_bias: bfloat16 [16384], P(('blk', 'red', 'sub')), may hold values from -0.5 to 0.5
- param_weight: bfloat16 [16384, 544], P(('blk', 'red', 'sub')), may hold values from -0.046875 to 0.046875
- step_gain: bfloat16 [512], replicated, may hold values from 0.25 to 1.75
- entry_gain: bfloat16 [16], replicated, may hold values from 0.099609375 to 1.8984375
- readout_gain: bfloat16 [16], replicated, may hold values from 0.099609375 to 1.8984375
- step_weight: bfloat16 [512, 16384], P(None, ('blk', 'red', 'sub')), may hold values from -0.25 to 0.25
- step_bias: float32 [16384], P(('blk', 'red', 'sub')), may hold values from -2 to 0.5
- decay_log: float32 [16, 16384], P(None, ('blk', 'red', 'sub')), may hold values from 0 to 2.77
- skip_gain: float32 [16384], P(('blk', 'red', 'sub')), may hold values from 0.5 to 1.5
- out_weight: bfloat16 [16384, 8192], P('blk', ('red', 'sub')), may hold values from -0.046875 to 0.046875
- conv_state: bfloat16 [3, 16384, 256], P(None, ('blk', 'red', 'sub'), 'grp'), parts along dimension 2, may hold values from -5 to 5
- scan_state: bfloat16 [16384, 16, 256], P(('blk', 'red', 'sub'), None, 'grp'), parts along dimension 2, may hold values from -5 to 5
Outputs:
- mixed: bfloat16 [256, 8192], P(('grp', 'blk'), ('red', 'sub')), parts along dimension 0
- new_conv: bfloat16 [3, 16384, 256], P(None, ('blk', 'red', 'sub'), 'grp'), parts along dimension 2
- new_scan: bfloat16 [16384, 16, 256], P(('blk', 'red', 'sub'), None, 'grp'), parts along dimension 2
There are 2 independent parts, one for each index of `grp`. A program takes and returns all parts, laid end to end along the dimension named above; an argument that names none is the same for every part. Nothing has to cross between parts.
All inputs are finite; a program needn't handle non-finite values.
Results may differ from a plain program's by a relative error of at most 0.03.
Values may be sent and summed in bfloat16 or wider, within the bound.
A program may use at most 128 MiB of HBM per device.

v0:
```python
import jax
import jax.numpy as jnp
from jax import lax
from jax.sharding import PartitionSpec as P


def contract(left, right, dims):
    return lax.dot_general(
        left.astype(jnp.float32),
        right.astype(jnp.float32),
        (dims, ((), ())),
        precision=lax.Precision.HIGHEST,
    )


def normalize(matrix, gain):
    return (
        matrix
        * lax.rsqrt(jnp.mean(matrix * matrix, axis=0, keepdims=True) + 1e-06)
        * gain.astype(jnp.float32)[:, None]
    )


def prenorm(rows_in, input_gain):
    wide = rows_in.astype(jnp.float32)
    scaled = wide * lax.rsqrt(jnp.mean(wide * wide, axis=1, keepdims=True) + 1e-06)
    return (scaled * input_gain.astype(jnp.float32)[None, :]).astype(jnp.bfloat16)


def split_params(summed, step_gain, entry_gain, readout_gain):
    width_low = step_gain.shape[0]
    width_state = entry_gain.shape[0]
    step_low = normalize(summed[:width_low], step_gain).astype(jnp.bfloat16)
    entry = normalize(summed[width_low : width_low + width_state], entry_gain).astype(jnp.bfloat16)
    readout = normalize(summed[width_low + width_state :], readout_gain).astype(jnp.bfloat16)
    return (step_low, entry, readout)


def body(
    tokens,
    input_gain,
    in_weight,
    conv_weight,
    conv_bias,
    param_weight,
    step_gain,
    entry_gain,
    readout_gain,
    step_weight,
    step_bias,
    decay_log,
    skip_gain,
    out_weight,
    conv_state,
    scan_state,
):
    all_rows = lax.all_gather(tokens, "blk", axis=0, tiled=True)
    full_rows = lax.all_gather(all_rows, ("red", "sub"), axis=1, tiled=True)
    row_piece = prenorm(full_rows, input_gain)
    first = contract(in_weight[0], row_piece, ((0,), (1,)))
    second = contract(in_weight[1], row_piece, ((0,), (1,)))
    projected = jnp.stack([first, second], axis=0)
    branch = projected[0].astype(jnp.bfloat16)
    gating = projected[1].astype(jnp.bfloat16)
    window = jnp.concatenate([conv_state, branch[None]], axis=0)
    new_conv = window[1:]
    convolved = (
        jnp.sum(window.astype(jnp.float32) * conv_weight.astype(jnp.float32)[:, :, None], axis=0)
        + conv_bias.astype(jnp.float32)[:, None]
    )
    activated = jax.nn.silu(convolved).astype(jnp.bfloat16)
    param_terms = contract(param_weight, activated, ((0,), (0,)))
    summed = lax.psum(param_terms, ("blk", "red", "sub"))
    step_low, entry, readout = split_params(summed, step_gain, entry_gain, readout_gain)
    step = jax.nn.softplus(contract(step_weight, step_low, ((0,), (0,))) + step_bias[:, None])
    active_wide = activated.astype(jnp.float32)
    rates = (-jnp.exp(decay_log)).T
    state = jnp.exp(step[:, None, :] * rates[:, :, None]) * scan_state.astype(jnp.float32)
    state = state + (step * active_wide)[:, None, :] * entry.astype(jnp.float32)[None, :, :]
    gated = (
        jnp.sum(state * readout.astype(jnp.float32)[None, :, :], axis=1)
        + skip_gain[:, None] * active_wide
    )
    gated = (gated * jax.nn.silu(gating.astype(jnp.float32))).astype(jnp.bfloat16)
    gathered = lax.all_gather(gated, ("red", "sub"), axis=0, tiled=True)
    output = lax.psum_scatter(
        contract(gathered, out_weight, ((0,), (0,))).astype(jnp.bfloat16),
        "blk",
        scatter_dimension=0,
        tiled=True,
    ).astype(jnp.float32)
    mixed = (tokens.astype(jnp.float32) + output).astype(jnp.bfloat16)
    return (mixed, new_conv, state.astype(jnp.bfloat16))


def solution(mesh):
    placed = (
        P(("grp", "blk"), ("red", "sub")),
        P(),
        P(None, None, ("blk", "red", "sub")),
        P(None, ("blk", "red", "sub")),
        P(("blk", "red", "sub")),
        P(("blk", "red", "sub"), None),
        P(),
        P(),
        P(),
        P(None, ("blk", "red", "sub")),
        P(("blk", "red", "sub")),
        P(None, ("blk", "red", "sub")),
        P(("blk", "red", "sub")),
        P("blk", ("red", "sub")),
        P(None, ("blk", "red", "sub"), "grp"),
        P(("blk", "red", "sub"), None, "grp"),
    )
    return jax.shard_map(
        body,
        mesh=mesh,
        in_specs=placed,
        out_specs=(
            P(("grp", "blk"), ("red", "sub")),
            P(None, ("blk", "red", "sub"), "grp"),
            P(("blk", "red", "sub"), None, "grp"),
        ),
        check_vma=False,
    )
```

profile of v0, /device:TPU:0, one launch (start us, length us, event | category | flops | bytes accessed | tf_op | source)
XLA Modules:
  0.0 258.1 jit_solution(16263312592786173018)
XLA Ops:
  7.2 0.7 all-gather.3.cloned.1.call-update
  8.0 26.5 %all-gather.3.cloned.1.call-done = bf16[128,4096]{1,0:T(8,128)(2,1)} async-done(((bf16[16,4096]{1,0:T(8,128)(2,1)}), bf16[128,4096]{1,0:T(8,128)(2,1)}) %all-gather.3.cloned.1.call-update) | async-done | bytes 1048592 | tf_op jit(solution)/shard_map/all_gather | solution.py:57
  34.5 0.7 convert_element_type.97
  35.2 0.7 convert_element_type.102
  35.9 0.7 convert_element_type.103
  37.9 0.7 convert_element_type.105
  38.6 30.1 %all-gather.5.cloned.1.call-done = bf16[128,8192]{1,0:T(8,128)(2,1)} async-done(((bf16[128,4096]{1,0:T(8,128)(2,1)}), bf16[128,8192]{1,0:T(8,128)(2,1)}) %all-gather.5.cloned.1.call-update) | async-done | bytes 2097168 | tf_op jit(solution)/shard_map/all_gather | solution.py:58
  68.8 2.1 fusion.7
  70.9 8.9 %fusion.23 = bf16[1,1024,128]{1,2,0:T(8,128)(2,1)S(1)} fusion(bf16[2,8192,1024]{2,1,0:T(8,128)(2,1)} %param.18, bf16[128,8192]{1,0:T(8,128)(2,1)} %all-gather.5.cloned.1.call-done, f32[8192]{0:T(1024)S(1)} %convert_element_type.97, f32[128]{0:T(128)S(1)} %add_rsqrt_fusion.3), kind=kOutput, calls=%fused_computation.26 | convolution fusion | flops 2151809024 | bytes 19169792 | tf_op jit(solution)/shard_map/dot_general | solution.py:8
  79.9 0.7 multiply_reduce_fusion.1
  80.9 1.2 convolution_bitcast_fusion
  82.4 89.3 %all-reduce.2.cloned.1.call-done = f32[544,128]{1,0:T(8,128)} async-done(((f32[544,128]{1,0:T(8,128)}), f32[544,128]{1,0:T(8,128)}) %all-reduce.2.cloned.1.call-update) | async-done | bytes 278544 | tf_op jit(solution)/shard_map/psum | solution.py:73
  171.7 1.0 multiply_reduce_fusion.2
  172.8 2.9 %convert_multiply_fusion.3 = (f32[1024,128]{0,1:T(8,128)}, f32[1024,128]{0,1:T(8,128)S(1)}) fusion(f32[1024,128]{0,1:T(8,128)S(1)} %copy.24, f32[1024]{0:T(1024)S(1)} %convert_element_type.103, f32[1024]{0:T(1024)S(1)} %copy-done.6, bf16[512,1024]{1,0:T(8,128)(2,1)} %param.25, f32[544,128]{1,0:T(8,128)} %all-reduce.2.cloned.1.call-done, ...), kind=kOutput, calls=%fused_computation.30 | convolution fusion | flops 136380416 | bytes 2894336 | tf_op jit(solution)/shard_map/dot_general | solution.py:8
  175.9 1.2 copy.27
  177.1 0.7 multiply_reduce_fusion.4
  177.9 0.8 fusion.38
  178.7 12.3 %fusion.6 = (bf16[1024,16,128]{2,1,0:T(8,128)(2,1)}, f32[1024,128]{1,0:T(8,128)S(1)}) fusion(bf16[1024,16,128]{2,1,0:T(8,128)(2,1)} %param.31, f32[16,128]{1,0:T(8,128)S(1)} %get-tuple-element.7, f32[1024,128]{1,0:T(8,128)S(1)} %copy.27, f32[1024,16]{1,0:T(8,128)S(1)} %copy.26, f32[1024,128]{1,0:T(8,128)S(1)} %copy.25, f32[16,128]{1,0:T(8,128)S(1)} %get-tuple-element.8), kind=kLoop, calls=%fused_computation.8 | loop fusion | flops 16646144 | bytes 10043392 | tf_op jit(solution)/shard_map/convert_element_type | solution.py:93
  191.2 9.0 %fusion.31 = bf16[1024,128]{0,1:T(8,128)(2,1)S(1)} fusion(f32[1024,128]{0,1:T(8,128)S(1)} %copy.28, bf16[2,8192,1024]{2,1,0:T(8,128)(2,1)} %param.18, bf16[128,8192]{1,0:T(8,128)(2,1)} %all-gather.5.cloned.1.call-done, f32[8192]{0:T(1024)S(1)} %convert_element_type.97, f32[128]{0:T(128)S(1)} %add_rsqrt_fusion.3, f32[1024]{0:T(1024)S(1)} %copy-done.7, ...), kind=kOutput, calls=%fused_computation.33 | convolution fusion | flops 2153906176 | bytes 20226560 | tf_op jit(solution)/shard_map/dot_general | solution.py:8
  200.2 8.9 %all_gather.11 = bf16[2048,128]{0,1:T(8,128)(2,1)S(1)} all-gather(bf16[1024,128]{0,1:T(8,128)(2,1)S(1)} %fusion.31), channel_id=1, replica_groups=mesh['grp'=2,'blk'=8,'red'=2,'sub'=1] {'red','sub'}, dimensions={0}, use_global_device_ids=true | all-gather | bytes 786432 | tf_op jit(solution)/shard_map/all_gather | solution.py:85
  209.1 9.2 %convolution_convert_fusion = bf16[128,4096]{1,0:T(8,128)(2,1)} fusion(bf16[2048,128]{0,1:T(8,128)(2,1)S(1)} %all_gather.11, bf16[2048,4096]{1,0:T(8,128)(2,1)} %param.29), kind=kOutput, calls=%fused_computation.11 | convolution fusion | flops 2148007936 | bytes 18350080 | tf_op jit(solution)/shard_map/dot_general | solution.py:8
  218.4 0.9 fusion.26
  219.3 30.6 %reduce-scatter.2.cloned.1.call-done = bf16[16,4096]{1,0:T(8,128)(2,1)} async-done(((bf16[128,4096]{1,0:T(8,128)(2,1)}), bf16[16,4096]{1,0:T(8,128)(2,1)}) %reduce-scatter.2.cloned.1.call-update) | async-done | bytes 131088 | tf_op jit(solution)/shard_map/reduce_scatter | solution.py:86
  249.9 1.6 add_convert_fusion
  (34 shorter events, 2.6 us)
Async XLA Ops:
  7.2 73.7 %copy-start = (bf16[1024,544]{0,1:T(8,128)(2,1)S(1)}, bf16[1024,544]{0,1:T(8,128)(2,1)}, u32[]{:S(2)}) copy-start(bf16[1024,544]{0,1:T(8,128)(2,1)} %param.21) | copy-start | bytes 3342340
  7.2 27.3 %all-gather.3.cloned.1.call-start = ((), (), s32[]{:S(2)}) async-start(), calls=%async_computation.1 | async-start | bytes 1179648 | tf_op jit(solution)/shard_map/all_gather | solution.py:57
  7.9 60.8 %all-gather.5.cloned.1.call-start = ((), (), s32[]{:S(2)}) async-start(), calls=%async_computation.2 | async-start | bytes 3145728 | tf_op jit(solution)/shard_map/all_gather | solution.py:58
  34.5 137.3 %all-reduce.2.cloned.1.call-start = ((), (), s32[]{:S(2)}) async-start(), calls=%async_computation.3 | async-start | bytes 557056 | tf_op jit(solution)/shard_map/psum | solution.py:73
  70.8 9.1 %copy-start.2 = (bf16[3,1024,128]{2,1,0:T(8,128)(2,1)S(1)}, bf16[3,1024,128]{2,1,0:T(8,128)(2,1)}, u32[]{:S(2)}) copy-start(bf16[3,1024,128]{2,1,0:T(8,128)(2,1)} %param.30) | copy-start | bytes 2359300
  79.7 2.5 copy-start.5
  79.7 93.0 %copy-start.6 = (f32[1024]{0:T(1024)S(1)}, f32[1024]{0:T(1024)}, u32[]{:S(2)}) copy-start(f32[1024]{0:T(1024)} %param.26) | copy-start | bytes 12292
  80.9 94.8 %copy-start.4 = (f32[1024,128]{0,1:T(8,128)}, f32[1024,128]{0,1:T(8,128)S(1)}, u32[]{:S(2)}) copy-start(f32[1024,128]{0,1:T(8,128)S(1)} %copy.24) | copy-start | bytes 1572868
  82.1 167.8 %reduce-scatter.2.cloned.1.call-start = ((), (), s32[]{:S(2)}) async-start(), calls=%async_computation.4 | async-start | bytes 1179648 | tf_op jit(solution)/shard_map/reduce_scatter | solution.py:86
  178.7 12.5 %copy-start.7 = (f32[1024]{0:T(1024)S(1)}, f32[1024]{0:T(1024)}, u32[]{:S(2)}) copy-start(f32[1024]{0:T(1024)} %param.28) | copy-start | bytes 12292
  209.1 40.8 %copy-start.3 = (bf16[16,4096]{1,0:T(8,128)(2,1)S(1)}, bf16[16,4096]{1,0:T(8,128)(2,1)}, u32[]{:S(2)}) copy-start(bf16[16,4096]{1,0:T(8,128)(2,1)} %param.16) | copy-start | bytes 393220
  209.1 42.4 %copy-start.1 = (bf16[1024,544]{0,1:T(8,128)(2,1)S(1)}, bf16[1024,544]{0,1:T(8,128)(2,1)}, u32[]{:S(2)}) copy-start(bf16[1024,544]{0,1:T(8,128)(2,1)} %param.21) | copy-start | bytes 3342340
Sparse Core Ops, SparseCore 0:
  9.6 24.7 all-gather.2
  36.0 32.7 all-gather.4
  82.3 89.4 all-reduce.1
  218.5 31.4 reduce-scatter.1
where the time goes:
time: 259 us; the launch traced here: 258 us
  waiting for transfers between devices  177 us (68%)
  matrix products  31.2 us (12%)
  other arithmetic  24.4 us (9%)
  between operations  13.9 us (5%)
  blocking collectives  8.9 us (3%)
    psum x1, waiting for transfers between devices, body(): summed = lax.psum(param_terms, ('blk', 'red', 'sub'))  89.3 us
    dot_general x5, matrix products, contract(): lax.dot_general(left.astype(jnp.float32), right.astype(jnp.float32), (dim...  31.2 us
    reduce_scatter x1, waiting for transfers between devices, body(): lax.psum_scatter(contract(gathered, out_weight, ((0,), (0,))).astype(jnp....  30.6 us
    all_gather x1, waiting for transfers between devices, body(): full_rows = lax.all_gather(all_rows, ('red', 'sub'), axis=1, tiled=True)  30.1 us
    all_gather x1, waiting for transfers between devices, body(): all_rows = lax.all_gather(tokens, 'blk', axis=0, tiled=True)  26.5 us
    convert_element_type x1, other arithmetic, body(): return (mixed, new_conv, state.astype(jnp.bfloat16))  12.3 us
    all_gather x1, blocking collectives, body(): gathered = lax.all_gather(gated, ('red', 'sub'), axis=0, tiled=True)  8.9 us
  transfers between devices with their start and end apart: 4, of which 4 were waited for; matrix products, arithmetic and copies ran while one was open for 2% of the time, Pallas kernels for 0%

commit v1 on v0

--- a/solution.py
+++ b/solution.py
@@ -6,10 +6,10 @@
 
 def contract(left, right, dims):
     return lax.dot_general(
-        left.astype(jnp.float32),
-        right.astype(jnp.float32),
+        left,
+        right,
         (dims, ((), ())),
-        precision=lax.Precision.HIGHEST,
+        preferred_element_type=jnp.float32,
     )
 
 

time: 259 us -> 259 us (level)
  no operation moved by 1% of the time
where the time goes in v1:
time: 259 us; the launch traced here: 258 us
  waiting for transfers between devices  177 us (68%)
  matrix products  31.2 us (12%)
  other arithmetic  24.4 us (9%)
  between operations  13.9 us (5%)
  blocking collectives  8.9 us (3%)
    psum x1, waiting for transfers between devices, body(): summed = lax.psum(param_terms, ('blk', 'red', 'sub'))  89.3 us
    dot_general x5, matrix products, contract(): lax.dot_general(left, right, (dims, ((), ())), preferred_element_type=jnp...  31.2 us
    reduce_scatter x1, waiting for transfers between devices, body(): lax.psum_scatter(contract(gathered, out_weight, ((0,), (0,))).astype(jnp....  30.6 us
    all_gather x1, waiting for transfers between devices, body(): full_rows = lax.all_gather(all_rows, ('red', 'sub'), axis=1, tiled=True)  30.1 us
    all_gather x1, waiting for transfers between devices, body(): all_rows = lax.all_gather(tokens, 'blk', axis=0, tiled=True)  26.5 us
    convert_element_type x1, other arithmetic, body(): return (mixed, new_conv, state.astype(jnp.bfloat16))  12.3 us
    all_gather x1, blocking collectives, body(): gathered = lax.all_gather(gated, ('red', 'sub'), axis=0, tiled=True)  8.9 us
  transfers between devices with their start and end apart: 4, of which 4 were waited for; matrix products, arithmetic and copies ran while one was open for 2% of the time, Pallas kernels for 0%

profile of v1, /device:TPU:0, one launch (start us, length us, event | category | flops | bytes accessed | tf_op | source)
XLA Modules:
  0.0 258.1 jit_solution(10938374428212681442)
XLA Ops:
  7.2 0.7 all-gather.3.cloned.1.call-update
  8.0 26.5 %all-gather.3.cloned.1.call-done = bf16[128,4096]{1,0:T(8,128)(2,1)} async-done(((bf16[16,4096]{1,0:T(8,128)(2,1)}), bf16[128,4096]{1,0:T(8,128)(2,1)}) %all-gather.3.cloned.1.call-update) | async-done | bytes 1048592 | tf_op jit(solution)/shard_map/all_gather | solution.py:57
  34.5 0.7 convert_element_type.87
  35.2 0.7 convert_element_type.92
  35.9 0.7 convert_element_type.93
  37.9 0.7 convert_element_type.95
  38.6 30.1 %all-gather.5.cloned.1.call-done = bf16[128,8192]{1,0:T(8,128)(2,1)} async-done(((bf16[128,4096]{1,0:T(8,128)(2,1)}), bf16[128,8192]{1,0:T(8,128)(2,1)}) %all-gather.5.cloned.1.call-update) | async-done | bytes 2097168 | tf_op jit(solution)/shard_map/all_gather | solution.py:58
  68.8 2.1 fusion.7
  70.9 8.9 %fusion.23 = bf16[1,1024,128]{1,2,0:T(8,128)(2,1)S(1)} fusion(bf16[2,8192,1024]{2,1,0:T(8,128)(2,1)} %param.18, bf16[128,8192]{1,0:T(8,128)(2,1)} %all-gather.5.cloned.1.call-done, f32[8192]{0:T(1024)S(1)} %convert_element_type.87, f32[128]{0:T(128)S(1)} %add_rsqrt_fusion.3), kind=kOutput, calls=%fused_computation.26 | convolution fusion | flops 2151809024 | bytes 19169792 | tf_op jit(solution)/shard_map/dot_general | solution.py:8
  79.9 0.7 multiply_reduce_fusion.1
  80.9 1.2 convolution_bitcast_fusion
  82.4 89.3 %all-reduce.2.cloned.1.call-done = f32[544,128]{1,0:T(8,128)} async-done(((f32[544,128]{1,0:T(8,128)}), f32[544,128]{1,0:T(8,128)}) %all-reduce.2.cloned.1.call-update) | async-done | bytes 278544 | tf_op jit(solution)/shard_map/psum | solution.py:73
  171.7 1.0 multiply_reduce_fusion.2
  172.8 2.9 %convert_multiply_fusion.3 = (f32[1024,128]{0,1:T(8,128)}, f32[1024,128]{0,1:T(8,128)S(1)}) fusion(f32[1024,128]{0,1:T(8,128)S(1)} %copy.24, f32[1024]{0:T(1024)S(1)} %convert_element_type.93, f32[1024]{0:T(1024)S(1)} %copy-done.6, bf16[512,1024]{1,0:T(8,128)(2,1)} %param.25, f32[544,128]{1,0:T(8,128)} %all-reduce.2.cloned.1.call-done, ...), kind=kOutput, calls=%fused_computation.30 | convolution fusion | flops 136380416 | bytes 2894336 | tf_op jit(solution)/shard_map/dot_general | solution.py:8
  175.9 1.2 copy.27
  177.1 0.7 multiply_reduce_fusion.4
  177.9 0.8 fusion.38
  178.7 12.3 %fusion.6 = (bf16[1024,16,128]{2,1,0:T(8,128)(2,1)}, f32[1024,128]{1,0:T(8,128)S(1)}) fusion(bf16[1024,16,128]{2,1,0:T(8,128)(2,1)} %param.31, f32[16,128]{1,0:T(8,128)S(1)} %get-tuple-element.7, f32[1024,128]{1,0:T(8,128)S(1)} %copy.27, f32[1024,16]{1,0:T(8,128)S(1)} %copy.26, f32[1024,128]{1,0:T(8,128)S(1)} %copy.25, f32[16,128]{1,0:T(8,128)S(1)} %get-tuple-element.8), kind=kLoop, calls=%fused_computation.8 | loop fusion | flops 16646144 | bytes 10043392 | tf_op jit(solution)/shard_map/convert_element_type | solution.py:93
  191.2 9.0 %fusion.31 = bf16[1024,128]{0,1:T(8,128)(2,1)S(1)} fusion(f32[1024,128]{0,1:T(8,128)S(1)} %copy.28, bf16[2,8192,1024]{2,1,0:T(8,128)(2,1)} %param.18, bf16[128,8192]{1,0:T(8,128)(2,1)} %all-gather.5.cloned.1.call-done, f32[8192]{0:T(1024)S(1)} %convert_element_type.87, f32[128]{0:T(128)S(1)} %add_rsqrt_fusion.3, f32[1024]{0:T(1024)S(1)} %copy-done.7, ...), kind=kOutput, calls=%fused_computation.33 | convolution fusion | flops 2153906176 | bytes 20226560 | tf_op jit(solution)/shard_map/dot_general | solution.py:8
  200.2 8.9 %all_gather.11 = bf16[2048,128]{0,1:T(8,128)(2,1)S(1)} all-gather(bf16[1024,128]{0,1:T(8,128)(2,1)S(1)} %fusion.31), channel_id=1, replica_groups=mesh['grp'=2,'blk'=8,'red'=2,'sub'=1] {'red','sub'}, dimensions={0}, use_global_device_ids=true | all-gather | bytes 786432 | tf_op jit(solution)/shard_map/all_gather | solution.py:85
  209.1 9.2 %convolution_convert_fusion = bf16[128,4096]{1,0:T(8,128)(2,1)} fusion(bf16[2048,128]{0,1:T(8,128)(2,1)S(1)} %all_gather.11, bf16[2048,4096]{1,0:T(8,128)(2,1)} %param.29), kind=kOutput, calls=%fused_computation.11 | convolution fusion | flops 2148007936 | bytes 18350080 | tf_op jit(solution)/shard_map/dot_general | solution.py:8
  218.4 0.9 fusion.26
  219.3 30.6 %reduce-scatter.2.cloned.1.call-done = bf16[16,4096]{1,0:T(8,128)(2,1)} async-done(((bf16[128,4096]{1,0:T(8,128)(2,1)}), bf16[16,4096]{1,0:T(8,128)(2,1)}) %reduce-scatter.2.cloned.1.call-update) | async-done | bytes 131088 | tf_op jit(solution)/shard_map/reduce_scatter | solution.py:86
  249.9 1.6 add_convert_fusion
  (34 shorter events, 2.6 us)
Async XLA Ops:
  7.2 73.7 %copy-start = (bf16[1024,544]{0,1:T(8,128)(2,1)S(1)}, bf16[1024,544]{0,1:T(8,128)(2,1)}, u32[]{:S(2)}) copy-start(bf16[1024,544]{0,1:T(8,128)(2,1)} %param.21) | copy-start | bytes 3342340
  7.2 27.3 %all-gather.3.cloned.1.call-start = ((), (), s32[]{:S(2)}) async-start(), calls=%async_computation.1 | async-start | bytes 1179648 | tf_op jit(solution)/shard_map/all_gather | solution.py:57
  7.9 60.8 %all-gather.5.cloned.1.call-start = ((), (), s32[]{:S(2)}) async-start(), calls=%async_computation.2 | async-start | bytes 3145728 | tf_op jit(solution)/shard_map/all_gather | solution.py:58
  34.5 137.3 %all-reduce.2.cloned.1.call-start = ((), (), s32[]{:S(2)}) async-start(), calls=%async_computation.3 | async-start | bytes 557056 | tf_op jit(solution)/shard_map/psum | solution.py:73
  70.8 9.1 %copy-start.2 = (bf16[3,1024,128]{2,1,0:T(8,128)(2,1)S(1)}, bf16[3,1024,128]{2,1,0:T(8,128)(2,1)}, u32[]{:S(2)}) copy-start(bf16[3,1024,128]{2,1,0:T(8,128)(2,1)} %param.30) | copy-start | bytes 2359300
  79.7 2.5 copy-start.5
  79.7 93.0 %copy-start.6 = (f32[1024]{0:T(1024)S(1)}, f32[1024]{0:T(1024)}, u32[]{:S(2)}) copy-start(f32[1024]{0:T(1024)} %param.26) | copy-start | bytes 12292
  80.9 94.8 %copy-start.4 = (f32[1024,128]{0,1:T(8,128)}, f32[1024,128]{0,1:T(8,128)S(1)}, u32[]{:S(2)}) copy-start(f32[1024,128]{0,1:T(8,128)S(1)} %copy.24) | copy-start | bytes 1572868
  82.1 167.8 %reduce-scatter.2.cloned.1.call-start = ((), (), s32[]{:S(2)}) async-start(), calls=%async_computation.4 | async-start | bytes 1179648 | tf_op jit(solution)/shard_map/reduce_scatter | solution.py:86
  178.7 12.5 %copy-start.7 = (f32[1024]{0:T(1024)S(1)}, f32[1024]{0:T(1024)}, u32[]{:S(2)}) copy-start(f32[1024]{0:T(1024)} %param.28) | copy-start | bytes 12292
  209.1 40.8 %copy-start.3 = (bf16[16,4096]{1,0:T(8,128)(2,1)S(1)}, bf16[16,4096]{1,0:T(8,128)(2,1)}, u32[]{:S(2)}) copy-start(bf16[16,4096]{1,0:T(8,128)(2,1)} %param.16) | copy-start | bytes 393220
  209.1 42.4 %copy-start.1 = (bf16[1024,544]{0,1:T(8,128)(2,1)S(1)}, bf16[1024,544]{0,1:T(8,128)(2,1)}, u32[]{:S(2)}) copy-start(bf16[1024,544]{0,1:T(8,128)(2,1)} %param.21) | copy-start | bytes 3342340
Sparse Core Ops, SparseCore 0:
  9.6 24.7 all-gather.2
  36.0 32.7 all-gather.4
  82.3 89.4 all-reduce.1
  218.5 31.4 reduce-scatter.1

commit v2 on v1

--- a/solution.py
+++ b/solution.py
@@ -1,6 +1,9 @@
+import functools
 import jax
 import jax.numpy as jnp
 from jax import lax
+from jax.experimental import pallas as pl
+from jax.experimental.pallas import tpu as pltpu
 from jax.sharding import PartitionSpec as P
 
 
@@ -93,7 +96,588 @@
     return (mixed, new_conv, state.astype(jnp.bfloat16))
 
 
+MESH = pl.DeviceIdType.MESH
+F32 = jnp.float32
+BF16 = jnp.bfloat16
+LANES = 128
+HALF = 384
+RING = 6
+PARTS = 4
+
+
+def silu(v):
+    return v / (1.0 + jnp.exp(-v))
+
+
+def softplus(v):
+    return jnp.maximum(v, 0.0) + jnp.log1p(jnp.exp(-jnp.abs(v)))
+
+
+def kernel(
+    blocks,
+    tokens,
+    gain,
+    in_w,
+    conv_w,
+    conv_b,
+    par_w,
+    step_gain,
+    entry_gain,
+    read_gain,
+    step_w,
+    step_b,
+    decay_log,
+    skip,
+    out_w,
+    conv_in,
+    scan_in,
+    mixed,
+    conv_out,
+    scan_out,
+    tok,
+    scaled,
+    squares,
+    iw,
+    acc,
+    pw,
+    sw,
+    ow,
+    conv,
+    branch,
+    scan,
+    small,
+    small_t,
+    rates,
+    act,
+    act_t,
+    gate,
+    step,
+    drive,
+    pp,
+    prv,
+    pall,
+    low,
+    inout,
+    dot_out,
+    heads,
+    part,
+    sib,
+    mine,
+    far,
+    mix,
+    load_sem,
+    iw_sem,
+    store_sem,
+    scan_sem,
+    tok_recv,
+    tok_z,
+    tok_x,
+    tok_sib,
+    par_send,
+    par_recv,
+    all_send,
+    all_recv,
+    head_send,
+    head_recv,
+    sib_send,
+    sib_recv,
+    far_send,
+    far_recv,
+):
+    g = lax.axis_index("grp")
+    b = lax.axis_index("blk")
+    x = lax.axis_index("red")
+    z = b // 2
+    c = b % 2
+    nz = blocks // 2
+    me = b * 2 + x
+    total = blocks * 2
+    rows = tokens.shape[0]
+    wide = tokens.shape[1]
+    seqs = rows * blocks
+    chan = act.shape[0]
+    kc = wide // PARTS
+    nblk = chan // LANES
+    twin = (g, b + 1 - 2 * c, x, 0)
+    peer = (g, b, 1 - x, 0)
+
+    def load(src, dst, at):
+        return pltpu.make_async_copy(src, dst, load_sem.at[at])
+
+    def weight(t):
+        h, j = t // PARTS, t % PARTS
+        start = ((x + h) % 2) * wide + j * kc
+        return pltpu.make_async_copy(
+            in_w.at[:, pl.ds(pl.multiple_of(start, kc), kc), :],
+            iw.at[t % RING],
+            iw_sem.at[t % RING],
+        )
+
+    def block_rows(at):
+        return pl.ds(pl.multiple_of(at * rows, rows), rows)
+
+    first = load(tokens, tok.at[x, block_rows(b)], 0)
+    first.start()
+    for t in range(RING):
+        weight(t).start()
+    get_conv = load(conv_in, conv, 1)
+    get_pw = load(par_w, pw, 2)
+    get_sw = load(step_w, sw, 3)
+    get_scan = load(scan_in, scan, 4)
+    get_ow = load(out_w, ow, 5)
+    get_conv.start()
+    get_pw.start()
+    get_sw.start()
+
+    barrier = pltpu.get_barrier_semaphore()
+
+    def partner(k):
+        idx = lax.rem(me + k, total)
+        return (g, idx // 2, idx % 2, 0), idx
+
+    def greet(k, carry):
+        pl.semaphore_signal(barrier, inc=1, device_id=partner(k)[0], device_id_type=MESH)
+        return carry
+
+    lax.fori_loop(1, total, greet, 0)
+    pl.semaphore_wait(barrier, total - 1)
+
+    def send(src, dst, ssem, rsem, where):
+        return pltpu.make_async_remote_copy(
+            src_ref=src, dst_ref=dst, send_sem=ssem, recv_sem=rsem, device_id=where, device_id_type=MESH
+        )
+
+    def tok_copy(half, blk, ssem, where):
+        ref = tok.at[half, block_rows(blk)]
+        return send(ref, ref, ssem, tok_recv.at[half, blk], where)
+
+    def to_z(k):
+        z_to = lax.rem(z + k, nz)
+        return tok_copy(x, b, tok_z.at[k], (g, z_to * 2 + c, x, 0))
+
+    def to_peer(k):
+        blk = lax.rem(z + k, nz) * 2 + c
+        return tok_copy(x, blk, tok_x.at[k], peer)
+
+    def to_twin(h, k):
+        blk = lax.rem(z + k, nz) * 2 + c
+        return tok_copy((x + h) % 2, blk, tok_sib.at[h, k], twin)
+
+    def got(half, blk):
+        ref = tok.at[half, block_rows(blk)]
+        send(ref, ref, tok_z.at[0], tok_recv.at[half, blk], peer).wait_recv()
+
+    first.wait()
+    to_peer(0).start()
+    for k in range(1, nz):
+        to_z(k).start()
+    to_twin(0, 0).start()
+
+    small[...] = jnp.zeros_like(small)
+    small[0:4, :] = conv_w[...].astype(F32)
+    small[4:5, :] = conv_b[...].astype(F32)
+    small[5:6, :] = step_b[...]
+    small[6:7, :] = skip[...]
+    rates[...] = -jnp.exp(decay_log[...])
+
+    def flip_small(i, carry):
+        at = pl.ds(pl.multiple_of(i * LANES, LANES), LANES)
+        small_t[at, :] = small[:, at].T
+        return carry
+
+    lax.fori_loop(0, nblk, flip_small, 0)
+    squares[...] = jnp.zeros_like(squares)
+    acc[...] = jnp.zeros_like(acc)
+    pp[...] = jnp.zeros_like(pp)
+
+    for k in range(1, nz):
+        got(x, lax.rem(z + k, nz) * 2 + c)
+        to_peer(k).start()
+        to_twin(0, k).start()
+
+    for h in range(2):
+        half = (x + h) % 2
+        if h == 1:
+            for k in range(nz):
+                got(half, lax.rem(z + k, nz) * 2 + c)
+                to_twin(1, k).start()
+        for k in range(nz):
+            got(half, lax.rem(z + k, nz) * 2 + 1 - c)
+
+        def scale(j, carry):
+            at = pl.ds(pl.multiple_of(j * LANES, LANES), LANES)
+            col = pl.ds(pl.multiple_of(half * wide + j * LANES, LANES), LANES)
+            v = tok[half, :, at].astype(F32)
+            squares[...] += v * v
+            scaled[:, at] = (v * gain[:, col].astype(F32)).astype(BF16)
+            return carry
+
+        lax.fori_loop(0, wide // LANES, scale, 0)
+
+        def project(j, carry):
+            t = h * PARTS + j
+            weight(t).wait()
+            lhs = scaled[:, pl.ds(pl.multiple_of(j * kc, kc), kc)]
+            slot = t % RING
+            for w in range(2):
+                acc[w] += jnp.dot(lhs, iw[slot, w], preferred_element_type=F32)
+
+            @pl.when(t + RING < 2 * PARTS)
+            def _():
+                weight(t + RING).start()
+
+            return carry
+
+        lax.fori_loop(0, PARTS, project, 0)
+        if h == 0:
+            get_scan.start()
+            get_ow.start()
+
+    inv = lax.rsqrt(jnp.sum(squares[...], axis=1, keepdims=True) / (2.0 * wide) + 1e-06)
+    get_conv.wait()
+
+    def convolve(i, carry):
+        at = pl.ds(pl.multiple_of(i * LANES, LANES), LANES)
+        br = (acc[0, :, at] * inv).T.astype(BF16)
+        branch[at, :] = br
+        cols = small_t[at, :]
+        v = br.astype(F32) * cols[:, 3:4]
+        for k in range(3):
+            v += conv[k, at, :].astype(F32) * cols[:, k : k + 1]
+        a = silu(v + cols[:, 4:5]).astype(BF16).astype(F32)
+        act[at, :] = a
+        act_t[:, at] = a.T.astype(BF16)
+        gt = (acc[1, :, at] * inv).T.astype(BF16).astype(F32)
+        gate[at, :] = silu(gt)
+        return carry
+
+    lax.fori_loop(0, nblk, convolve, 0)
+    put_conv = pltpu.make_async_copy(conv.at[pl.ds(1, 2)], conv_out.at[pl.ds(0, 2)], store_sem.at[0])
+    put_branch = pltpu.make_async_copy(branch, conv_out.at[2], store_sem.at[1])
+    put_conv.start()
+    put_branch.start()
+
+    get_pw.wait()
+    width = pw.shape[1]
+    terms = jnp.dot(act_t[...], pw[...], preferred_element_type=F32).astype(BF16)
+    pp[0] = terms[:, 0:HALF].reshape(blocks, rows, HALF)
+    dot_out[...] = jnp.zeros_like(dot_out)
+    dot_out[:, 0 : width - HALF] = terms[:, HALF:width]
+    pp[1] = dot_out[...].reshape(blocks, rows, HALF)
+
+    def par_copy(k):
+        where, idx = partner(k)
+        return send(pp.at[idx % 2, idx // 2], prv.at[me], par_send.at[k], par_recv.at[me], where)
+
+    def all_copy(k):
+        where, idx = partner(k)
+        ref = pall.at[x, b]
+        return send(ref, ref, all_send.at[k], all_recv.at[me], where)
+
+    def start_par(k, carry):
+        par_copy(k).start()
+        return carry
+
+    lax.fori_loop(1, total, start_par, 0)
+
+    def take_par(k, summed):
+        where, idx = partner(k)
+        send(prv.at[idx], prv.at[idx], par_send.at[0], par_recv.at[idx], where).wait_recv()
+        return summed + prv[idx].astype(F32)
+
+    summed = lax.fori_loop(1, total, take_par, pp[x, b].astype(F32))
+    pall[x, b] = summed.astype(BF16)
+
+    def start_all(k, carry):
+        all_copy(k).start()
+        return carry
+
+    lax.fori_loop(1, total, start_all, 0)
+    get_sw.wait()
+    get_scan.wait()
+
+    def take_all(k, carry):
+        where, idx = partner(k)
+        ref = pall.at[idx % 2, idx // 2]
+        send(ref, ref, all_send.at[0], all_recv.at[idx], where).wait_recv()
+        return carry
+
+    lax.fori_loop(1, total, take_all, 0)
+
+    one = pall[0].astype(F32).reshape(seqs, HALF)
+    two = pall[1].astype(F32).reshape(seqs, HALF)
+    rank = step_gain.shape[1]
+    extra = two[:, 0 : rank - HALF]
+    norm = lax.rsqrt(
+        (jnp.sum(one * one, axis=1, keepdims=True) + jnp.sum(extra * extra, axis=1, keepdims=True)) / rank
+        + 1e-06
+    )
+    gains = step_gain[...].astype(F32)
+    low[:, 0:HALF] = (one * norm * gains[:, 0:HALF]).astype(BF16)
+    low[:, HALF:rank] = (extra * norm * gains[:, HALF:rank]).astype(BF16)
+    flipped = two[:, rank - HALF : rank - HALF + LANES].T
+    states = entry_gain.shape[0]
+
+    def short(v, weights):
+        v = v * lax.rsqrt(jnp.mean(v * v, axis=0, keepdims=True) + 1e-06) * weights[...].astype(F32)
+        return v.astype(BF16).astype(F32)
+
+    inout[0] = short(flipped[0:states], entry_gain)
+    inout[1] = short(flipped[states : 2 * states], read_gain)
+
+    def head_copy(i):
+        at = pl.ds(pl.multiple_of(x * chan + i * LANES, LANES), LANES)
+        ref = heads.at[:, at]
+        return send(ref, ref, head_send.at[i], head_recv.at[i], peer)
+
+    def head_got(i):
+        at = pl.ds(pl.multiple_of((1 - x) * chan + i * LANES, LANES), LANES)
+        ref = heads.at[:, at]
+        send(ref, ref, head_send.at[i], head_recv.at[i], peer).wait_recv()
+
+    def put_scan(i):
+        at = pl.ds(pl.multiple_of(i * LANES, LANES), LANES)
+        return pltpu.make_async_copy(scan.at[at], scan_out.at[at], scan_sem.at[i])
+
+    def advance(i, carry):
+        base = pl.multiple_of(i * LANES, LANES)
+        at = pl.ds(base, LANES)
+        cols = small_t[at, :]
+        raw = jnp.dot(low[...], sw[:, at], preferred_element_type=F32).T
+        st = softplus(raw + cols[:, 5:6])
+        step[...] = st
+        drive[...] = st * act[at, :]
+        decay = rates[:, at]
+
+        def group(q, inner):
+            rolled = pltpu.roll(decay, LANES - q * 8, 1)
+            entry = inout[0]
+            readout = inout[1]
+            for j in range(8):
+                e = q * 8 + j
+                fade = jnp.exp(step[pl.ds(e, 1), :] * rolled[:, j : j + 1])
+                state = fade * scan[base + e].astype(F32) + drive[pl.ds(e, 1), :] * entry
+                scan[base + e] = state.astype(BF16)
+                step[pl.ds(e, 1), :] = jnp.sum(state * readout, axis=0, keepdims=True)
+            return inner
+
+        lax.fori_loop(0, LANES // 8, group, 0)
+        put_scan(i).start()
+        out = (step[...] + cols[:, 6:7] * act[at, :]) * gate[at, :]
+        heads[:, pl.ds(pl.multiple_of(x * chan + i * LANES, LANES), LANES)] = out.T.astype(BF16)
+        head_copy(i).start()
+        return carry
+
+    lax.fori_loop(0, nblk, advance, 0)
+    get_ow.wait()
+
+    def wait_heads(i, carry):
+        head_got(i)
+        return carry
+
+    lax.fori_loop(0, nblk, wait_heads, 0)
+
+    def sib_copy(n):
+        return send(part.at[n, :, 1 - c], sib.at[n], sib_send.at[n], sib_recv.at[n], twin)
+
+    def far_copy(n, k):
+        z_to = lax.rem(z + k, nz)
+        return send(
+            mine.at[n, z_to], far.at[n, k], far_send.at[n, k], far_recv.at[n, k], (g, z_to * 2 + c, x, 0)
+        )
+
+    for n in range(PARTS + 1):
+        if n < PARTS:
+            p = jnp.dot(heads[...], ow[:, n * kc : (n + 1) * kc], preferred_element_type=F32)
+            part[n] = p.astype(BF16).reshape(nz, 2, rows, kc)
+            sib_copy(n).start()
+        if n > 0:
+            m = n - 1
+            sib_copy(m).wait_recv()
+            mine[m] = (part[m, :, c].astype(F32) + sib[m].astype(F32)).astype(BF16)
+            for k in range(1, nz):
+                far_copy(m, k).start()
+
+    for n in range(PARTS):
+        v = mine[n, z].astype(F32)
+        for k in range(1, nz):
+            far_copy(n, k).wait_recv()
+            v += far[n, k].astype(F32)
+        at = slice(n * kc, (n + 1) * kc)
+        own = tok[x, block_rows(b), at].astype(F32)
+        mix[:, at] = (own + v).astype(BF16)
+    put_mix = pltpu.make_async_copy(mix, mixed, store_sem.at[2])
+    put_mix.start()
+
+    for k in range(nz):
+        to_peer(k).wait_send()
+        to_twin(0, k).wait_send()
+        to_twin(1, k).wait_send()
+    for k in range(1, nz):
+        to_z(k).wait_send()
+
+    def drain(k, carry):
+        par_copy(k).wait_send()
+        all_copy(k).wait_send()
+        return carry
+
+    lax.fori_loop(1, total, drain, 0)
+
+    def drain_blocks(i, carry):
+        head_copy(i).wait_send()
+        put_scan(i).wait()
+        return carry
+
+    lax.fori_loop(0, nblk, drain_blocks, 0)
+    for n in range(PARTS):
+        sib_copy(n).wait_send()
+        for k in range(1, nz):
+            far_copy(n, k).wait_send()
+    put_conv.wait()
+    put_branch.wait()
+    put_mix.wait()
+
+
+def fused(
+    blocks,
+    tokens,
+    input_gain,
+    in_weight,
+    conv_weight,
+    conv_bias,
+    param_weight,
+    step_gain,
+    entry_gain,
+    readout_gain,
+    step_weight,
+    step_bias,
+    decay_log,
+    skip_gain,
+    out_weight,
+    conv_state,
+    scan_state,
+):
+    rows, wide = tokens.shape
+    seqs = rows * blocks
+    chan = in_weight.shape[2]
+    rank = step_gain.shape[0]
+    states = entry_gain.shape[0]
+    nz = blocks // 2
+    kc = wide // PARTS
+    nblk = chan // LANES
+    total = 2 * blocks
+    vm = pl.BlockSpec(memory_space=pltpu.VMEM)
+    hbm = pl.BlockSpec(memory_space=pl.ANY)
+    dma = pltpu.SemaphoreType.DMA
+    v = pltpu.VMEM
+    scratch = [
+        v((2, seqs, wide), BF16),
+        v((seqs, wide), BF16),
+        v((seqs, LANES), F32),
+        v((RING, 2, kc, chan), BF16),
+        v((2, seqs, chan), F32),
+        v(param_weight.shape, BF16),
+        v(step_weight.shape, BF16),
+        v(out_weight.shape, BF16),
+        v(conv_state.shape, BF16),
+        v((chan, seqs), BF16),
+        v(scan_state.shape, BF16),
+        v((LANES, chan), F32),
+        v((chan, LANES), F32),
+        v((states, chan), F32),
+        v((chan, seqs), F32),
+        v((seqs, chan), BF16),
+        v((chan, seqs), F32),
+        v((LANES, seqs), F32),
+        v((LANES, seqs), F32),
+        v((2, blocks, rows, HALF), BF16),
+        v((total, rows, HALF), BF16),
+        v((2, blocks, rows, HALF), BF16),
+        v((seqs, rank), BF16),
+        v((2, states, seqs), F32),
+        v((seqs, HALF), BF16),
+        v((seqs, 2 * chan), BF16),
+        v((PARTS, nz, 2, rows, kc), BF16),
+        v((PARTS, nz, rows, kc), BF16),
+        v((PARTS, nz, rows, kc), BF16),
+        v((PARTS, nz, rows, kc), BF16),
+        v((rows, wide), BF16),
+        dma((6,)),
+        dma((RING,)),
+        dma((3,)),
+        dma((nblk,)),
+        dma((2, blocks)),
+        dma((nz,)),
+        dma((nz,)),
+        dma((2, nz)),
+        dma((total,)),
+        dma((total,)),
+        dma((total,)),
+        dma((total,)),
+        dma((nblk,)),
+        dma((nblk,)),
+        dma((PARTS,)),
+        dma((PARTS,)),
+        dma((PARTS, nz)),
+        dma((PARTS, nz)),
+    ]
+    return pl.pallas_call(
+        functools.partial(kernel, blocks),
+        out_shape=(
+            jax.ShapeDtypeStruct(tokens.shape, BF16),
+            jax.ShapeDtypeStruct(conv_state.shape, BF16),
+            jax.ShapeDtypeStruct(scan_state.shape, BF16),
+        ),
+        in_specs=[hbm, vm, hbm, vm, vm, hbm, vm, vm, vm, hbm, vm, vm, vm, hbm, hbm, hbm],
+        out_specs=(hbm, hbm, hbm),
+        scratch_shapes=scratch,
+        compiler_params=pltpu.CompilerParams(
+            collective_id=0, has_side_effects=True, vmem_limit_bytes=62 * 1024 * 1024
+        ),
+    )(
+        tokens,
+        input_gain[None, :],
+        in_weight,
+        conv_weight,
+        conv_bias[None, :],
+        param_weight,
+        step_gain[None, :],
+        entry_gain[:, None],
+        readout_gain[:, None],
+        step_weight,
+        step_bias[None, :],
+        decay_log,
+        skip_gain[None, :],
+        out_weight,
+        conv_state,
+        scan_state,
+    )
+
+
+def fits(mesh, tokens, in_weight, step_gain, entry_gain, conv_weight):
+    rows, wide = tokens.shape
+    width = step_gain.shape[0] + 2 * entry_gain.shape[0]
+    return (
+        mesh.shape["sub"] == 1
+        and mesh.shape["red"] == 2
+        and mesh.shape["blk"] % 2 == 0
+        and rows == 16
+        and rows * mesh.shape["blk"] == LANES
+        and in_weight.shape[2] % LANES == 0
+        and wide % (PARTS * LANES) == 0
+        and HALF < step_gain.shape[0] == HALF + LANES
+        and width <= 2 * HALF
+        and entry_gain.shape[0] == 16
+        and conv_weight.shape[0] == 4
+    )
+
+
 def solution(mesh):
+    def chosen(*args):
+        if fits(mesh, args[0], args[2], args[6], args[7], args[3]):
+            return fused(mesh.shape["blk"], *args)
+        return body(*args)
+
     placed = (
         P(("grp", "blk"), ("red", "sub")),
         P(),
@@ -113,7 +697,7 @@
         P(("blk", "red", "sub"), None, "grp"),
     )
     return jax.shard_map(
-        body,
+        chosen,
         mesh=mesh,
         in_specs=placed,
         out_specs=(

time: 259 us -> 113 us (0.44)
  waiting for transfers between devices: 177 us -> 0 us
  Pallas kernels: 0 us -> 94.9 us
  matrix products: 31.2 us -> 0 us
  other arithmetic: 24.4 us -> 0 us
  local copies, waits for them, and re-layouts: 2.22 us -> 17.5 us
  between operations: 13.9 us -> 0.64 us
  blocking collectives: 8.9 us -> 0 us
    pallas_call x0 -> x1, Pallas kernels: none -> 94.9 us  [fused(): pl.pallas_call(functools.partial(kernel, blocks), out_shape=(jax.ShapeDty...]
    psum x1 -> x0, waiting for transfers between devices: 89.3 us -> none  [body(): summed = lax.psum(param_terms, ('blk', 'red', 'sub'))]
    all_gather x2 -> x0, waiting for transfers between devices: 56.6 us -> none  [the longest x1 30.1 us: body(): full_rows = lax.all_gather(all_rows, ('red', 'sub'), axis=1, tiled=True)]
    dot_general x5 -> x0, matrix products: 31.2 us -> none  [contract(): lax.dot_general(left, right, (dims, ((), ())), preferred_element_type=jnp...]
    reduce_scatter x1 -> x0, waiting for transfers between devices: 30.6 us -> none  [body(): lax.psum_scatter(contract(gathered, out_weight, ((0,), (0,))).astype(jnp....]
    convert_element_type x9 -> x0, other arithmetic: 18.8 us -> none  [the longest x1 12.3 us: body(): return (mixed, new_conv, state.astype(jnp.bfloat16))]
    unnamed x16 -> x4, local copies, waits for them, and re-layouts: 0.05 us -> 10.9 us
    all_gather x1 -> x0, blocking collectives: 8.9 us -> none  [body(): gathered = lax.all_gather(gated, ('red', 'sub'), axis=0, tiled=True)]
  transfers between devices with their start and end apart: 4 -> 0, of which waited for: 4 -> 0; matrix products, arithmetic and copies ran while one was open for 2% -> 0% of each run, Pallas kernels for 0% -> 0%
where the time goes in v2:
time: 113 us
  Pallas kernels  94.9 us (84%)
  local copies, waits for them, and re-layouts  17.5 us (15%)
    pallas_call x1, Pallas kernels, fused(): pl.pallas_call(functools.partial(kernel, blocks), out_shape=(jax.ShapeDty...  94.9 us
    unnamed x4, local copies, waits for them, and re-layouts  10.9 us

profile of v2, /device:TPU:0, one launch (start us, length us, event | category | flops | bytes accessed | tf_op | source)
XLA Modules:
  0.0 113.1 jit_solution(14340331366826931813)
XLA Ops:
  0.6 1.3 %broadcast_in_dim.23.step_gain = bf16[1,512]{1,0:T(2,128)(2,1)} reshape(bf16[512]{0:T(512)(128)(2,1)} %param.22) | data formatting | bytes 2048 | tf_op jit(solution)/shard_map/broadcast_in_dim | solution.py:644
  1.9 1.3 %broadcast_in_dim.22.conv_b = bf16[1,1024]{1,0:T(2,128)(2,1)} reshape(bf16[1024]{0:T(1024)(128)(2,1)} %param.20) | data formatting | bytes 4096 | tf_op jit(solution)/shard_map/broadcast_in_dim | solution.py:642
  3.2 1.3 %copy.20.entry_gain = bf16[16,1]{1,0:T(8,128)(2,1)} copy(bf16[16,1]{0,1:T(2,128)(2,1)} %bitcast.6) | data formatting | bytes 64 | tf_op jit(solution)/shard_map/broadcast_in_dim | solution.py:645
  4.5 1.3 %copy.21.read_gain = bf16[16,1]{1,0:T(8,128)(2,1)} copy(bf16[16,1]{0,1:T(2,128)(2,1)} %bitcast.7) | data formatting | bytes 64 | tf_op jit(solution)/shard_map/broadcast_in_dim | solution.py:646
  5.8 1.3 %broadcast_in_dim.21.gain = bf16[1,8192]{1,0:T(2,128)(2,1)} reshape(bf16[8192]{0:T(1024)(128)(2,1)} %param.17) | data formatting | bytes 32768 | tf_op jit(solution)/shard_map/broadcast_in_dim | solution.py:639
  7.2 2.4 %copy.19.par_w = bf16[1024,544]{1,0:T(8,128)(2,1)} copy(bf16[1024,544]{0,1:T(8,128)(2,1)} %param.21) | data formatting | bytes 2228224 | tf_op args[5]
  9.6 94.9 %shard_map.175 = (bf16[16,4096]{1,0:T(8,128)(2,1)}, bf16[3,1024,128]{2,1,0:T(8,128)(2,1)}, bf16[1024,16,128]{2,1,0:T(8,128)(2,1)}) custom-call(bf16[16,4096]{1,0:T(8,128)(2,1)} %tokens.1, bf16[1,8192]{1,0:T(2,128)(2,1)} %broadcast_in_dim.21.gain, bf16[2,8192,1024]{2,1,0:T(8,128)(2,1)} %in_w.1, bf16[4,1024]{1,0:T(4,128)(2,1)} %conv_w.1, ...), custom_call_target="tpu_custom_call" | custom-call | tf_op jit(solution)/shard_map/pallas_call | solution.py:624
  104.5 1.6 %copy.25 = bf16[16,4096]{1,0:T(8,128)(2,1)} copy(bf16[16,4096]{1,0:T(8,128)(2,1)} %get-tuple-element.6) | data formatting | bytes 262144
  106.1 2.1 %copy.26 = bf16[3,1024,128]{2,1,0:T(8,128)(2,1)} copy(bf16[3,1024,128]{2,1,0:T(8,128)(2,1)} %get-tuple-element.7) | data formatting | bytes 1572864
  108.2 4.9 %copy.27 = bf16[1024,16,128]{2,1,0:T(8,128)(2,1)} copy(bf16[1024,16,128]{2,1,0:T(8,128)(2,1)} %get-tuple-element.8) | data formatting | bytes 8388608

commit v3 on v2

--- a/solution.py
+++ b/solution.py
@@ -116,18 +116,11 @@
 def kernel(
     blocks,
     tokens,
-    gain,
+    packed,
     in_w,
-    conv_w,
-    conv_b,
     par_w,
-    step_gain,
-    entry_gain,
-    read_gain,
     step_w,
-    step_b,
     decay_log,
-    skip,
     out_w,
     conv_in,
     scan_in,
@@ -145,6 +138,7 @@
     conv,
     branch,
     scan,
+    gain_row,
     small,
     small_t,
     rates,
@@ -274,10 +268,9 @@
     to_twin(0, 0).start()
 
     small[...] = jnp.zeros_like(small)
-    small[0:4, :] = conv_w[...].astype(F32)
-    small[4:5, :] = conv_b[...].astype(F32)
-    small[5:6, :] = step_b[...]
-    small[6:7, :] = skip[...]
+    small[0:8, :] = packed[0:8, :]
+    for j in range(2 * wide // chan):
+        gain_row[:, j * chan : (j + 1) * chan] = packed[8 + j : 9 + j, :]
     rates[...] = -jnp.exp(decay_log[...])
 
     def flip_small(i, carry):
@@ -306,10 +299,10 @@
 
         def scale(j, carry):
             at = pl.ds(pl.multiple_of(j * LANES, LANES), LANES)
-            col = pl.ds(pl.multiple_of(half * wide + j * LANES, LANES), LANES)
+            gain = gain_row[:, pl.ds(pl.multiple_of(half * wide + j * LANES, LANES), LANES)]
             v = tok[half, :, at].astype(F32)
             squares[...] += v * v
-            scaled[:, at] = (v * gain[:, col].astype(F32)).astype(BF16)
+            scaled[:, at] = (v * gain).astype(BF16)
             return carry
 
         lax.fori_loop(0, wide // LANES, scale, 0)
@@ -358,8 +351,10 @@
     put_branch.start()
 
     get_pw.wait()
-    width = pw.shape[1]
-    terms = jnp.dot(act_t[...], pw[...], preferred_element_type=F32).astype(BF16)
+    width = pw.shape[0]
+    terms = lax.dot_general(
+        act_t[...], pw[...], (((1,), (1,)), ((), ())), preferred_element_type=F32
+    ).astype(BF16)
     pp[0] = terms[:, 0:HALF].reshape(blocks, rows, HALF)
     dot_out[...] = jnp.zeros_like(dot_out)
     dot_out[:, 0 : width - HALF] = terms[:, HALF:width]
@@ -406,24 +401,23 @@
 
     one = pall[0].astype(F32).reshape(seqs, HALF)
     two = pall[1].astype(F32).reshape(seqs, HALF)
-    rank = step_gain.shape[1]
+    rank = low.shape[1]
     extra = two[:, 0 : rank - HALF]
     norm = lax.rsqrt(
         (jnp.sum(one * one, axis=1, keepdims=True) + jnp.sum(extra * extra, axis=1, keepdims=True)) / rank
         + 1e-06
     )
-    gains = step_gain[...].astype(F32)
+    at_rank = 8 + 2 * wide // chan
+    gains = packed[at_rank : at_rank + 1, 0:rank]
     low[:, 0:HALF] = (one * norm * gains[:, 0:HALF]).astype(BF16)
     low[:, HALF:rank] = (extra * norm * gains[:, HALF:rank]).astype(BF16)
     flipped = two[:, rank - HALF : rank - HALF + LANES].T
-    states = entry_gain.shape[0]
-
-    def short(v, weights):
-        v = v * lax.rsqrt(jnp.mean(v * v, axis=0, keepdims=True) + 1e-06) * weights[...].astype(F32)
-        return v.astype(BF16).astype(F32)
-
-    inout[0] = short(flipped[0:states], entry_gain)
-    inout[1] = short(flipped[states : 2 * states], read_gain)
+    states = inout.shape[1]
+    for k in range(2):
+        at = slice(k * states, (k + 1) * states)
+        v = flipped[at]
+        v = v * lax.rsqrt(jnp.mean(v * v, axis=0, keepdims=True) + 1e-06) * small_t[at, 7:8]
+        inout[k] = v.astype(BF16).astype(F32)
 
     def head_copy(i):
         at = pl.ds(pl.multiple_of(x * chan + i * LANES, LANES), LANES)
@@ -453,12 +447,20 @@
             rolled = pltpu.roll(decay, LANES - q * 8, 1)
             entry = inout[0]
             readout = inout[1]
+            at8 = pl.ds(pl.multiple_of(q * 8, 8), 8)
+            at_scan = pl.ds(pl.multiple_of(base + q * 8, 8), 8)
+            times = step[at8, :]
+            drives = drive[at8, :]
+            olds = scan[at_scan]
+            news = []
+            sums = []
             for j in range(8):
-                e = q * 8 + j
-                fade = jnp.exp(step[pl.ds(e, 1), :] * rolled[:, j : j + 1])
-                state = fade * scan[base + e].astype(F32) + drive[pl.ds(e, 1), :] * entry
-                scan[base + e] = state.astype(BF16)
-                step[pl.ds(e, 1), :] = jnp.sum(state * readout, axis=0, keepdims=True)
+                fade = jnp.exp(times[j : j + 1] * rolled[:, j : j + 1])
+                state = fade * olds[j].astype(F32) + drives[j : j + 1] * entry
+                news.append(state.astype(BF16)[None])
+                sums.append(jnp.sum(state * readout, axis=0, keepdims=True))
+            scan[at_scan] = jnp.concatenate(news, axis=0)
+            step[at8, :] = jnp.concatenate(sums, axis=0)
             return inner
 
         lax.fori_loop(0, LANES // 8, group, 0)
@@ -576,12 +578,13 @@
         v((seqs, LANES), F32),
         v((RING, 2, kc, chan), BF16),
         v((2, seqs, chan), F32),
-        v(param_weight.shape, BF16),
+        v(param_weight.shape[::-1], BF16),
         v(step_weight.shape, BF16),
         v(out_weight.shape, BF16),
         v(conv_state.shape, BF16),
         v((chan, seqs), BF16),
         v(scan_state.shape, BF16),
+        v((1, 2 * wide), F32),
         v((LANES, chan), F32),
         v((chan, LANES), F32),
         v((states, chan), F32),
@@ -621,6 +624,19 @@
         dma((PARTS, nz)),
         dma((PARTS, nz)),
     ]
+    gains = jnp.concatenate([entry_gain, readout_gain]).astype(F32)
+    packed = jnp.concatenate(
+        [
+            conv_weight.astype(F32),
+            conv_bias.astype(F32)[None],
+            step_bias[None],
+            skip_gain[None],
+            jnp.pad(gains, (0, chan - 2 * states))[None],
+            input_gain.astype(F32).reshape(2 * wide // chan, chan),
+            jnp.pad(step_gain.astype(F32), (0, chan - rank))[None],
+        ],
+        axis=0,
+    )
     return pl.pallas_call(
         functools.partial(kernel, blocks),
         out_shape=(
@@ -628,7 +644,7 @@
             jax.ShapeDtypeStruct(conv_state.shape, BF16),
             jax.ShapeDtypeStruct(scan_state.shape, BF16),
         ),
-        in_specs=[hbm, vm, hbm, vm, vm, hbm, vm, vm, vm, hbm, vm, vm, vm, hbm, hbm, hbm],
+        in_specs=[hbm, vm, hbm, hbm, hbm, vm, hbm, hbm, hbm],
         out_specs=(hbm, hbm, hbm),
         scratch_shapes=scratch,
         compiler_params=pltpu.CompilerParams(
@@ -636,18 +652,11 @@
         ),
     )(
         tokens,
-        input_gain[None, :],
+        packed,
         in_weight,
-        conv_weight,
-        conv_bias[None, :],
-        param_weight,
-        step_gain[None, :],
-        entry_gain[:, None],
-        readout_gain[:, None],
+        param_weight.T,
         step_weight,
-        step_bias[None, :],
         decay_log,
-        skip_gain[None, :],
         out_weight,
         conv_state,
         scan_state,
@@ -665,6 +674,8 @@
         and rows * mesh.shape["blk"] == LANES
         and in_weight.shape[2] % LANES == 0
         and wide % (PARTS * LANES) == 0
+        and in_weight.shape[2] >= step_gain.shape[0]
+        and 2 * wide % in_weight.shape[2] == 0
         and HALF < step_gain.shape[0] == HALF + LANES
         and width <= 2 * HALF
         and entry_gain.shape[0] == 16

time: 113 us -> 109 us (0.965)
  local copies, waits for them, and re-layouts: 17.5 us -> 11.9 us
  other arithmetic: 0 us -> 2.11 us
    broadcast_in_dim x5 -> x0, local copies, waits for them, and re-layouts: 6.56 us -> none  [the longest x1 1.35 us: fused(): input_gain[None, :]]
    concatenate x0 -> x1, local copies, waits for them, and re-layouts: none -> 2.61 us  [fused(): jnp.concatenate([conv_weight.astype(F32), conv_bias.astype(F32)[None], st...]
    unnamed x4 -> x3, local copies, waits for them, and re-layouts: 10.9 us -> 8.55 us
    broadcast_in_dim x0 -> x3, other arithmetic: none -> 2.11 us  [the longest x1 0.75 us: fused(): jnp.pad(gains, (0, chan - 2 * states))[None]]
where the time goes in v3:
time: 109 us
  Pallas kernels  94 us (86%)
  local copies, waits for them, and re-layouts  11.9 us (11%)
  other arithmetic  2.11 us (2%)
    pallas_call x1, Pallas kernels, fused(): pl.pallas_call(functools.partial(kernel, blocks), out_shape=(jax.ShapeDty...  94 us
    unnamed x3, local copies, waits for them, and re-layouts  8.55 us
    concatenate x1, local copies, waits for them, and re-layouts, fused(): jnp.concatenate([conv_weight.astype(F32), conv_bias.astype(F32)[None], st...  2.61 us

profile of v3, /device:TPU:0, one launch (start us, length us, event | category | flops | bytes accessed | tf_op | source)
XLA Modules:
  0.0 108.7 jit_solution(9737253466272303979)
XLA Ops:
  0.6 0.7 broadcast_in_dim.32
  1.3 0.7 pad_convert_fusion
  2.0 0.7 fusion.3
  2.7 0.7 reshape.17
  3.5 2.6 %concatenate.7.packed = f32[17,1024]{1,0:T(8,128)} concatenate(bf16[4,1024]{1,0:T(4,128)(2,1)} %param.19, f32[1,1024]{1,0:T(1,128)S(1)} %bitcast.9, f32[1,1024]{1,0:T(1,128)} %bitcast.10, f32[1,1024]{1,0:T(1,128)} %bitcast.11, f32[1,1024]{1,0:T(1,128)S(1)} %bitcast.8, f32[8,1024]{1,0:T(8,128)S(1)} %reshape.17, f32[1,1024]{1,0:T(1,128)S(1)} %bitcast.7), dimensions={0} | concatenate | bytes 131072 | tf_op jit(solution)/shard_map/concatenate | solution.py:628
  6.1 94.0 %shard_map.175 = (bf16[16,4096]{1,0:T(8,128)(2,1)}, bf16[3,1024,128]{2,1,0:T(8,128)(2,1)}, bf16[1024,16,128]{2,1,0:T(8,128)(2,1)}) custom-call(bf16[16,4096]{1,0:T(8,128)(2,1)} %tokens.1, f32[17,1024]{1,0:T(8,128)} %concatenate.7.packed, bf16[2,8192,1024]{2,1,0:T(8,128)(2,1)} %in_w.1, bf16[544,1024]{1,0:T(8,128)(2,1)} %bitcast.6, bf16[512,1024]{1,0:T(8,128)(2,1)} %step_w.1, ...), custom_call_target="tpu_custom_call" | custom-call | tf_op jit(solution)/shard_map/pallas_call | solution.py:640
  100.1 1.6 %copy.22 = bf16[16,4096]{1,0:T(8,128)(2,1)} copy(bf16[16,4096]{1,0:T(8,128)(2,1)} %get-tuple-element.6) | data formatting | bytes 262144
  101.7 2.1 %copy.23 = bf16[3,1024,128]{2,1,0:T(8,128)(2,1)} copy(bf16[3,1024,128]{2,1,0:T(8,128)(2,1)} %get-tuple-element.7) | data formatting | bytes 1572864
  103.7 4.9 %copy.24 = bf16[1024,16,128]{2,1,0:T(8,128)(2,1)} copy(bf16[1024,16,128]{2,1,0:T(8,128)(2,1)} %get-tuple-element.8) | data formatting | bytes 8388608

commit v4 on v3

--- a/solution.py
+++ b/solution.py
@@ -442,6 +442,7 @@
         step[...] = st
         drive[...] = st * act[at, :]
         decay = rates[:, at]
+        place = lax.broadcasted_iota(jnp.int32, (8, seqs), 0)
 
         def group(q, inner):
             rolled = pltpu.roll(decay, LANES - q * 8, 1)
@@ -458,9 +459,16 @@
                 fade = jnp.exp(times[j : j + 1] * rolled[:, j : j + 1])
                 state = fade * olds[j].astype(F32) + drives[j : j + 1] * entry
                 news.append(state.astype(BF16)[None])
-                sums.append(jnp.sum(state * readout, axis=0, keepdims=True))
+                seen = state * readout
+                sums.append(seen[0:8] + seen[8:16])
             scan[at_scan] = jnp.concatenate(news, axis=0)
-            step[at8, :] = jnp.concatenate(sums, axis=0)
+            for shift in (1, 2, 4):
+                keep = (place // shift) % 2 == 0
+                sums = [
+                    jnp.where(keep, left, right) + pltpu.roll(jnp.where(keep, right, left), shift, 0)
+                    for left, right in zip(sums[0::2], sums[1::2])
+                ]
+            step[at8, :] = sums[0]
             return inner
 
         lax.fori_loop(0, LANES // 8, group, 0)

time: 109 us -> 109 us (level)
  no operation moved by 1% of the time
where the time goes in v4:
time: 109 us
  Pallas kernels  94.1 us (86%)
  local copies, waits for them, and re-layouts  11.9 us (11%)
  other arithmetic  2.11 us (2%)
    pallas_call x1, Pallas kernels, fused(): pl.pallas_call(functools.partial(kernel, blocks), out_shape=(jax.ShapeDty...  94.1 us
    unnamed x3, local copies, waits for them, and re-layouts  8.55 us
    concatenate x1, local copies, waits for them, and re-layouts, fused(): jnp.concatenate([conv_weight.astype(F32), conv_bias.astype(F32)[None], st...  2.61 us

profile of v4, /device:TPU:0, one launch (start us, length us, event | category | flops | bytes accessed | tf_op | source)
XLA Modules:
  0.0 108.7 jit_solution(1867228503417679697)
XLA Ops:
  0.6 0.7 broadcast_in_dim.32
  1.3 0.7 pad_convert_fusion
  2.0 0.7 fusion.3
  2.7 0.7 reshape.17
  3.5 2.6 %concatenate.7.packed = f32[17,1024]{1,0:T(8,128)} concatenate(bf16[4,1024]{1,0:T(4,128)(2,1)} %param.19, f32[1,1024]{1,0:T(1,128)S(1)} %bitcast.9, f32[1,1024]{1,0:T(1,128)} %bitcast.10, f32[1,1024]{1,0:T(1,128)} %bitcast.11, f32[1,1024]{1,0:T(1,128)S(1)} %bitcast.8, f32[8,1024]{1,0:T(8,128)S(1)} %reshape.17, f32[1,1024]{1,0:T(1,128)S(1)} %bitcast.7), dimensions={0} | concatenate | bytes 131072 | tf_op jit(solution)/shard_map/concatenate | solution.py:636
  6.1 94.1 %shard_map.175 = (bf16[16,4096]{1,0:T(8,128)(2,1)}, bf16[3,1024,128]{2,1,0:T(8,128)(2,1)}, bf16[1024,16,128]{2,1,0:T(8,128)(2,1)}) custom-call(bf16[16,4096]{1,0:T(8,128)(2,1)} %tokens.1, f32[17,1024]{1,0:T(8,128)} %concatenate.7.packed, bf16[2,8192,1024]{2,1,0:T(8,128)(2,1)} %in_w.1, bf16[544,1024]{1,0:T(8,128)(2,1)} %bitcast.6, bf16[512,1024]{1,0:T(8,128)(2,1)} %step_w.1, ...), custom_call_target="tpu_custom_call" | custom-call | tf_op jit(solution)/shard_map/pallas_call | solution.py:648
  100.2 1.6 %copy.22 = bf16[16,4096]{1,0:T(8,128)(2,1)} copy(bf16[16,4096]{1,0:T(8,128)(2,1)} %get-tuple-element.6) | data formatting | bytes 262144
  101.8 2.1 %copy.23 = bf16[3,1024,128]{2,1,0:T(8,128)(2,1)} copy(bf16[3,1024,128]{2,1,0:T(8,128)(2,1)} %get-tuple-element.7) | data formatting | bytes 1572864
  103.8 4.9 %copy.24 = bf16[1024,16,128]{2,1,0:T(8,128)(2,1)} copy(bf16[1024,16,128]{2,1,0:T(8,128)(2,1)} %get-tuple-element.8) | data formatting | bytes 8388608
